TPU v7x, 32 devices: a whole 2x2x4 slice. The times are simulated.
32 devices in a mesh: dp: 4 (over x, core), fsdp: 4 (over z), seq: 2 (over y).
Axes of the slice: x: 2, y: 2, z: 4, core: 2. Of those that a mesh axis runs over, the one named last changes fastest.
Arguments:
- frames: bfloat16 [16, 512, 1536], P(('dp', 'fsdp'), 'seq'), may hold values from -6 to 6
- projection: bfloat16 [1536, 3072], P('fsdp'), may hold values from -1 to 1
- lengths: int32 [16], P(('dp', 'fsdp')), may hold values from 128 to 512
- cotangent: bfloat16 [16, 512, 1024], P(('dp', 'fsdp'), 'seq'), may hold values from -24 to 24
Outputs:
- context: bfloat16 [16, 512, 1024], P(('dp', 'fsdp'), 'seq')
- input_gradient: float32 [16, 512, 1536], P(('dp', 'fsdp'), 'seq')
- projection_gradient: float32 [1536, 3072], P(('dp', 'fsdp', 'seq'))
All inputs are finite; a program needn't handle non-finite values.
Results may differ from a plain program's by a relative error of at most 0.007.
The roundings to bfloat16 on the way count: a program that leaves them out, or rounds other values in their place, can miss the bound.
Values may be sent and summed in bfloat16 or wider, within the bound.
A program may use at most 128 MiB of HBM per device.

v0:
```python
import math

import jax
import jax.numpy as jnp
from jax import lax
from jax.sharding import PartitionSpec as P

HEADS = 16
HD = 64


EPS = 1e-05


def block_probabilities(query_block, key_rows, valid):
    factor = 1.0 / math.sqrt(query_block.shape[-1])
    scores = (
        jnp.einsum("qhd,khd->hqk", query_block, key_rows, preferred_element_type=jnp.float32)
        * factor
    )
    scores = jnp.where(valid[None, None, :], scores, -jnp.inf)
    row_peak = jnp.max(scores, axis=2, keepdims=True)
    exponentials = jnp.exp(scores - row_peak)
    return exponentials / jnp.sum(exponentials, axis=2, keepdims=True)


def forward_heads(query_rows, key_rows, value_rows, valid, block_rows):
    total_rows = query_rows.shape[0]

    def forward_one_block(block_index):
        first_row = block_index * block_rows
        query_block = lax.dynamic_slice_in_dim(query_rows, first_row, block_rows, 0)
        probabilities = block_probabilities(query_block, key_rows, valid)
        mixture = jnp.einsum(
            "hqk,khd->qhd",
            probabilities.astype(jnp.bfloat16),
            value_rows,
            preferred_element_type=jnp.float32,
        )
        keep_rows = lax.dynamic_slice_in_dim(valid, first_row, block_rows, 0)
        return jnp.where(keep_rows[:, None, None], mixture, jnp.zeros_like(mixture)).astype(
            jnp.bfloat16
        )

    blocks = lax.map(forward_one_block, jnp.arange(total_rows // block_rows, dtype=jnp.int32))
    return blocks.reshape(query_rows.shape)


def backward_heads(query_rows, key_rows, value_rows, upstream, valid, block_rows):
    total_rows = query_rows.shape[0]
    factor = 1.0 / math.sqrt(query_rows.shape[-1])

    def backward_one_block(running, block_index):
        key_sum, value_sum = running
        first_row = block_index * block_rows
        query_block = lax.dynamic_slice_in_dim(query_rows, first_row, block_rows, 0)
        upstream_block = lax.dynamic_slice_in_dim(upstream, first_row, block_rows, 0)
        keep_rows = lax.dynamic_slice_in_dim(valid, first_row, block_rows, 0)
        upstream_block = jnp.where(
            keep_rows[:, None, None], upstream_block, jnp.zeros_like(upstream_block)
        )
        probabilities = block_probabilities(query_block, key_rows, valid)
        value_sum = value_sum + jnp.einsum(
            "hqk,qhd->khd",
            probabilities.astype(jnp.bfloat16),
            upstream_block,
            preferred_element_type=jnp.float32,
        )
        prob_gradient = jnp.einsum(
            "qhd,khd->hqk", upstream_block, value_rows, preferred_element_type=jnp.float32
        )
        row_inner = jnp.sum(probabilities * prob_gradient, axis=2, keepdims=True)
        score_gradient = (probabilities * (prob_gradient - row_inner) * factor).astype(jnp.bfloat16)
        query_gradient = jnp.einsum(
            "hqk,khd->qhd", score_gradient, key_rows, preferred_element_type=jnp.float32
        ).astype(jnp.bfloat16)
        key_sum = key_sum + jnp.einsum(
            "hqk,qhd->khd", score_gradient, query_block, preferred_element_type=jnp.float32
        )
        return ((key_sum, value_sum), query_gradient)

    empty_sum = jnp.zeros(key_rows.shape, jnp.float32)
    sums, query_blocks = lax.scan(
        backward_one_block,
        (empty_sum, empty_sum),
        jnp.arange(total_rows // block_rows, dtype=jnp.int32),
    )
    return (
        query_blocks.reshape(query_rows.shape),
        sums[0].astype(jnp.bfloat16),
        sums[1].astype(jnp.bfloat16),
    )


def body(frames, projection, lengths, cotangent):
    inputs = frames[0]
    upstream = cotangent[0]
    length = lengths[0]
    seq_count = lax.axis_size("seq")
    local_rows, feature_count = inputs.shape
    total_rows = local_rows * seq_count
    head_count = HEADS // seq_count
    group_width = head_count * HD
    block_rows = 512
    as_float = inputs.astype(jnp.float32)
    centered = as_float - jnp.mean(as_float, axis=1, keepdims=True)
    inv_std = lax.rsqrt(jnp.mean(centered * centered, axis=1, keepdims=True) + EPS)
    standard = centered * inv_std
    normed = standard.astype(jnp.bfloat16)
    valid = jnp.arange(total_rows, dtype=jnp.int32) < length
    weight_full = lax.all_gather(projection, "fsdp", axis=0, tiled=True)
    packed = jnp.dot(normed, weight_full, preferred_element_type=jnp.float32).astype(jnp.bfloat16)
    packed = packed.reshape(local_rows, 3, seq_count, group_width)
    upstream_four = upstream.reshape(local_rows, 1, seq_count, group_width)
    head_inputs, head_upstream = (
        lax.all_to_all(packed, "seq", split_axis=2, concat_axis=0, tiled=True),
        lax.all_to_all(upstream_four, "seq", split_axis=2, concat_axis=0, tiled=True),
    )
    head_inputs = head_inputs.reshape(total_rows, 3, head_count, HD)
    head_grads = head_upstream.reshape(total_rows, head_count, HD)
    query_rows = head_inputs[:, 0]
    key_rows = head_inputs[:, 1]
    value_rows = head_inputs[:, 2]
    mixture = forward_heads(query_rows, key_rows, value_rows, valid, block_rows)
    returned_context = lax.all_to_all(
        mixture.reshape(total_rows, 1, group_width), "seq", split_axis=0, concat_axis=1, tiled=True
    )
    context = returned_context.reshape(local_rows, seq_count * group_width)
    query_gradient, key_gradient, value_gradient = backward_heads(
        query_rows, key_rows, value_rows, head_grads, valid, block_rows
    )
    stacked = jnp.stack([query_gradient, key_gradient, value_gradient], axis=1).reshape(
        total_rows, 3, 1, group_width
    )
    returned = lax.all_to_all(stacked, "seq", split_axis=0, concat_axis=2, tiled=True)
    packed_gradient = returned.reshape(local_rows, 3 * seq_count * group_width)
    normed_gradient = lax.dot_general(
        packed_gradient, weight_full, (((1,), (1,)), ((), ())), preferred_element_type=jnp.float32
    )
    projection_gradient = lax.psum_scatter(
        lax.dot_general(
            normed, packed_gradient, (((0,), (0,)), ((), ())), preferred_element_type=jnp.float32
        ),
        ("dp", "fsdp", "seq"),
        scatter_dimension=0,
        tiled=True,
    )
    row_mean = jnp.mean(normed_gradient, axis=1, keepdims=True)
    projected = jnp.mean(normed_gradient * standard, axis=1, keepdims=True)
    input_gradient = inv_std * (normed_gradient - row_mean - standard * projected)
    return (context[None], input_gradient[None], projection_gradient)


def solution(mesh):
    placed = (
        P(("dp", "fsdp"), "seq", None),
        P("fsdp", None),
        P(("dp", "fsdp")),
        P(("dp", "fsdp"), "seq", None),
    )
    return jax.shard_map(
        body,
        mesh=mesh,
        in_specs=placed,
        out_specs=(
            P(("dp", "fsdp"), "seq", None),
            P(("dp", "fsdp"), "seq", None),
            P(("dp", "fsdp", "seq"), None),
        ),
        check_vma=False,
    )
```

profile of v0, /device:TPU:0, one launch (start us, length us, event | category | flops | bytes accessed | tf_op | source)
XLA Modules:
  0.0 521.8 jit_solution(15757583872548408027)
XLA Ops:
  7.2 0.0 all-gather.2.cloned.1.call-start
  7.2 0.7 all-gather.2.cloned.1.call-update
  7.9 1.2 copy.83
  9.2 1.0 copy.84
  10.2 4.2 all-to-all-start.2
  14.4 0.2 convert_reduce_fusion
  14.6 0.4 fusion.29
  15.0 164.1 %all-gather.2.cloned.1.call-done = bf16[1536,3072]{1,0:T(8,128)(2,1)} async-done(((bf16[384,3072]{1,0:T(8,128)(2,1)}), bf16[1536,3072]{1,0:T(8,128)(2,1)}) %all-gather.2.cloned.1.call-update) | async-done | bytes 9437200 | tf_op jit(solution)/shard_map/all_gather | solution.py:111
  179.1 7.7 %convolution_convert_fusion = bf16[256,3072]{1,0:T(8,128)(2,1)} fusion(bf16[1536,3072]{1,0:T(8,128)(2,1)} %all-gather.2.cloned.1.call-done, bf16[1,256,1536]{2,1,0:T(8,128)(2,1)S(1)} %copy-done, f32[256]{0:T(256)S(1)} %add_rsqrt_fusion, f32[256]{0:T(256)S(1)} %broadcast_multiply_fusion.2), kind=kOutput, calls=%fused_computation.14 | convolution fusion | flops 2418278400 | bytes 11798528 | tf_op jit(solution)/shard_map/dot_general | solution.py:112
  186.7 4.0 reshape.78
  190.8 1.4 copy.78
  192.2 0.0 all-to-all-done.2
  192.2 3.7 all-to-all-start
  195.9 0.2 reduce-scatter.2.cloned.1.call-start
  196.8 0.5 copy.85
  197.2 0.3 reshape.80
  197.6 18.0 %all-to-all-done = bf16[256,3,2,512]{3,0,1,2:T(8,128)(2,1)S(1)} async-done(((bf16[256,3,2,512]{3,0,1,2:T(8,128)(2,1)}), bf16[256,3,2,512]{3,0,1,2:T(8,128)(2,1)S(1)}, u32[]{:S(2)}, u32[]{:S(2)}) %all-to-all-start) | async-done | bytes 1572896 | tf_op jit(solution)/shard_map/all_to_all | solution.py:116
  215.6 2.9 copy.79
  218.4 2.8 reshape.79
  221.2 0.0 copy-start.1
  221.2 5.3 %fusion.70 = (f32[8,512]{1,0:T(8,128)S(1)}, f32[8,512,512]{1,2,0:T(8,128)}) fusion(pred[512]{0:T(512)(128)(4,1)S(1)} %iota_compare_fusion, bf16[512,3,8,64]{0,3,2,1:T(8,128)(2,1)S(1)} %reshape.79), kind=kOutput, calls=%fused_computation.70 | convolution fusion | flops 276824576 | bytes 9454080 | tf_op jit(solution)/shard_map/while/body/eval_jaxpr/sub | solution.py:23
  226.5 5.4 %fusion.57 = f32[8,512,512]{1,2,0:T(8,128)} fusion(bf16[512,3,8,64]{0,3,2,1:T(8,128)(2,1)S(1)} %reshape.79, bf16[512,8,64]{0,2,1:T(8,128)(2,1)S(1)} %reshape.80, pred[512]{0:T(512)(128)(4,1)S(1)} %iota_compare_fusion), kind=kOutput, calls=%fused_computation.52 | convolution fusion | flops 268697600 | bytes 9437696 | tf_op jit(solution)/shard_map/while/body/eval_jaxpr/qhd,khd->hqk/dot_general | solution.py:69
  231.9 0.7 copy-done.3
  232.6 2.2 fusion.38
  234.7 15.2 %fusion.41 = bf16[8,64,512]{2,1,0:T(8,128)(2,1)} fusion(f32[8,512,512]{1,2,0:T(8,128)} %fusion.57, bf16[512,3,8,64]{0,3,2,1:T(8,128)(2,1)S(1)} %reshape.79, f32[8,512,512]{1,2,0:T(8,128)} %get-tuple-element.48, f32[8,512]{1,0:T(8,128)S(1)} %get-tuple-element.47), kind=kOutput, calls=%fused_computation.39 | convolution fusion | flops 283382272 | bytes 34635776 | tf_op jit(solution)/shard_map/while/body/eval_jaxpr/hqk,khd->qhd/dot_general | solution.py:74
  250.0 12.4 %fusion.44 = bf16[8,64,512]{2,1,0:T(8,128)(2,1)S(1)} fusion(f32[8,512,512]{1,2,0:T(8,128)} %fusion.57, bf16[512,3,8,64]{0,3,2,1:T(8,128)(2,1)S(1)} %reshape.79, f32[8,512,512]{1,2,0:T(8,128)} %get-tuple-element.48, f32[8,512]{1,0:T(8,128)S(1)} %get-tuple-element.47), kind=kOutput, calls=%fused_computation.40 | convolution fusion | flops 283382272 | bytes 34635776 | tf_op jit(solution)/shard_map/while/body/eval_jaxpr/hqk,qhd->khd/dot_general | solution.py:77
  262.4 0.9 copy.91
  263.3 2.4 copy.89
  265.7 2.0 copy.90
  267.7 4.7 pad_maximum_fusion
  272.4 27.0 %all_to_all.60 = bf16[512,3,1,512]{3,1,2,0:T(4,128)(2,1)S(1)} all-to-all(bf16[512,3,1,512]{3,1,2,0:T(4,128)(2,1)S(1)} %pad_maximum_fusion), channel_id=1, replica_groups=mesh['dp'=4,'fsdp'=4,'seq'=2] {'seq'}, dimensions={0} | all-to-all | bytes 3145728 | tf_op jit(solution)/shard_map/all_to_all | solution.py:135
  299.4 1.5 copy.92
  301.0 1.7 copy.93
  302.7 8.1 %fusion.50 = f32[1536,3072]{1,0:T(8,128)} fusion(bf16[256,3072]{0,1:T(8,128)(2,1)S(1)} %bitcast.95, bf16[1,256,1536]{2,1,0:T(8,128)(2,1)S(1)} %copy-done, f32[256]{0:T(256)S(1)} %add_rsqrt_fusion, f32[256]{0:T(256)S(1)} %broadcast_multiply_fusion.2), kind=kOutput, calls=%fused_computation.43 | convolution fusion | flops 2417491968 | bytes 21235712 | tf_op jit(solution)/shard_map/dot_general | solution.py:141
  310.7 0.0 reduce-scatter.2.cloned.1.call-update
  310.8 4.8 fusion.35
  315.6 0.5 broadcast.101
  316.1 1.0 reduce.1
  317.2 0.2 copy.100
  317.4 0.4 reshape.82
  317.8 9.7 %all_to_all.61 = bf16[2,2,65536]{2,1,0:T(2,128)(2,1)} all-to-all(bf16[2,2,65536]{2,1,0:T(2,128)(2,1)S(1)} %reshape.82), channel_id=1, replica_groups=mesh['dp'=4,'fsdp'=4,'seq'=2] {'seq'}, dimensions={0} | all-to-all | bytes 1048576 | tf_op jit(solution)/shard_map/all_to_all | solution.py:125
  327.5 1.4 reshape.83
  329.0 0.9 copy.99
  329.9 1.3 copy.82
  331.1 1.0 copy.94
  332.1 6.1 %fusion.69 = (f32[256]{0:T(256)S(1)}, f32[256]{0:T(256)S(1)}, f32[256,1536]{1,0:T(8,128)S(1)}) fusion(f32[256]{0:T(256)S(1)} %add_rsqrt_fusion, f32[256]{0:T(256)S(1)} %broadcast_multiply_fusion.2, bf16[1,256,1536]{2,1,0:T(8,128)(2,1)S(1)} %copy-done, bf16[256,3072]{0,1:T(8,128)(2,1)S(1)} %bitcast.96, bf16[1536,3072]{1,0:T(8,128)(2,1)} %all-gather.2.cloned.1.call-done), kind=kOutput, calls=%fused_computation.69 | convolution fusion | flops 2418277888 | bytes 13373440 | tf_op jit(solution)/shard_map/dot_general | solution.py:137
  338.3 1.6 fusion.28
  339.9 175.0 %reduce-scatter.2.cloned.1.call-done = f32[48,3072]{1,0:T(8,128)} async-done(((f32[1536,3072]{1,0:T(8,128)}), f32[48,3072]{1,0:T(8,128)}) %reduce-scatter.2.cloned.1.call-update) | async-done | bytes 589840 | tf_op jit(solution)/shard_map/reduce_scatter | solution.py:140
  (10 shorter events, 0.0 us)
Async XLA Ops:
  7.2 7.2 %copy-start = (bf16[1,256,1536]{2,1,0:T(8,128)(2,1)S(1)}, bf16[1,256,1536]{2,1,0:T(8,128)(2,1)}, u32[]{:S(2)}) copy-start(bf16[1,256,1536]{2,1,0:T(8,128)(2,1)} %param.4) | copy-start | bytes 2359300
  7.2 171.9 %all-gather.2.cloned.1.call-start = ((), (), s32[]{:S(2)}) async-start(), calls=%async_computation.5 | async-start | bytes 11796480 | tf_op jit(solution)/shard_map/all_gather | solution.py:111
  10.2 182.0 %all-to-all-start.2 = ((bf16[256,1,2,512]{3,0,1,2:T(8,128)(2,1)}), bf16[256,1,2,512]{3,0,1,2:T(8,128)(2,1)S(1)}, u32[]{:S(2)}, u32[]{:S(2)}) async-start(bf16[256,1,2,512]{3,0,1,2:T(8,128)(2,1)} %copy.84), calls=%async_computation.2 | async-start | bytes 1048576 | tf_op jit(solution)/shard_map/all_to_all | solution.py:117
  192.2 23.4 %all-to-all-start = ((bf16[256,3,2,512]{3,0,1,2:T(8,128)(2,1)}), bf16[256,3,2,512]{3,0,1,2:T(8,128)(2,1)S(1)}, u32[]{:S(2)}, u32[]{:S(2)}) async-start(bf16[256,3,2,512]{3,0,1,2:T(8,128)(2,1)} %copy.78), calls=%async_computation | async-start | bytes 3145728 | tf_op jit(solution)/shard_map/all_to_all | solution.py:116
  195.9 319.1 %reduce-scatter.2.cloned.1.call-start = ((), (), s32[]{:S(2)}) async-start(), calls=%async_computation.6 | async-start | bytes 19464192 | tf_op jit(solution)/shard_map/reduce_scatter | solution.py:140
  221.2 28.8 %copy-start.1 = (bf16[512,3,8,64]{0,3,2,1:T(8,128)(2,1)}, bf16[512,3,8,64]{0,3,2,1:T(8,128)(2,1)S(1)}, u32[]{:S(2)}) copy-start(bf16[512,3,8,64]{0,3,2,1:T(8,128)(2,1)S(1)} %reshape.79) | copy-start | bytes 4718596
  226.5 6.1 %copy-start.3 = (f32[8,512,512]{1,2,0:T(8,128)S(1)}, f32[8,512,512]{1,2,0:T(8,128)}, u32[]{:S(2)}) copy-start(f32[8,512,512]{1,2,0:T(8,128)} %get-tuple-element.48) | copy-start | bytes 25165828
  250.0 12.4 %copy-start.2 = (bf16[8,64,512]{2,1,0:T(8,128)(2,1)S(1)}, bf16[8,64,512]{2,1,0:T(8,128)(2,1)}, u32[]{:S(2)}) copy-start(bf16[8,64,512]{2,1,0:T(8,128)(2,1)} %fusion.38) | copy-start | bytes 1572868
Sparse Core Ops, SparseCore 0:
  9.6 169.4 all-gather.1
  310.9 204.0 reduce-scatter.1
where the time goes:
time: 523 us; the launch traced here: 522 us
  waiting for transfers between devices  358 us (68%)
  matrix products  67.1 us (13%)
  blocking collectives  36.7 us (7%)
  local copies, waits for them, and re-layouts  29.1 us (6%)
  between operations  14.9 us (3%)
  starting transfers between devices  8.17 us (2%)
  other arithmetic  7.91 us (2%)
    reduce_scatter x1, waiting for transfers between devices, body(): lax.psum_scatter(lax.dot_general(normed, packed_gradient, (((0,), (0,)),...  175 us
    all_gather x1, waiting for transfers between devices, body(): weight_full = lax.all_gather(projection, 'fsdp', axis=0, tiled=True)  164 us
    all_to_all x1, blocking collectives, body(): lax.all_to_all(stacked, 'seq', split_axis=0, concat_axis=2, tiled=True)  27 us
    all_to_all x1, waiting for transfers between devices, body(): lax.all_to_all(packed, 'seq', split_axis=2, concat_axis=0, tiled=True)  18 us
    dot_general x1, matrix products, backward_one_block(): jnp.einsum('hqk,khd->qhd', score_gradient, key_rows, preferred_element_ty...  15.2 us
    dot_general x1, matrix products, backward_one_block(): jnp.einsum('hqk,qhd->khd', score_gradient, query_block, preferred_element...  12.4 us
  transfers between devices with their start and end apart: 4, of which 3 were waited for; matrix products, arithmetic and copies ran while one was open for 7% of the time, Pallas kernels for 0%

commit v1 on v0

v1 whole, which is shorter than its diff:
```python
import functools
import math

import jax
import jax.numpy as jnp
from jax import lax
from jax.experimental import pallas as pl
from jax.experimental.pallas import tpu as pltpu
from jax.sharding import PartitionSpec as P

HEADS = 16
HD = 64
EPS = 1e-05
MESH = pl.DeviceIdType.MESH
F32 = jnp.float32
BF16 = jnp.bfloat16
VMEM_BYTES = 56 * 1024 * 1024


def ring(axis, step):
    size = lax.axis_size(axis)
    return lax.rem(lax.axis_index(axis) + step + size, size)


def greet(seq_count, fsdp_count, dp):
    barrier = pltpu.get_barrier_semaphore()
    for peer in (dp ^ 1, dp ^ 2):
        pl.semaphore_signal(barrier, inc=1, device_id={"dp": peer}, device_id_type=MESH)
    for d in range(1, fsdp_count):
        pl.semaphore_signal(barrier, inc=1, device_id={"fsdp": ring("fsdp", d)}, device_id_type=MESH)
    for d in range(1, seq_count):
        pl.semaphore_signal(barrier, inc=1, device_id={"seq": ring("seq", d)}, device_id_type=MESH)
    pl.semaphore_wait(barrier, 2 + fsdp_count - 1 + seq_count - 1)


def gather_kernel(
    seq_count, fsdp_count, w_ref, x_ref, c_ref, w_all, x_all, c_all,
    local_sem, xs, xr, cs, cr, zs, zr, f1s, f1r, f2s, f2r, f3s, f3r,
):
    dp = lax.axis_index("dp")
    fs = lax.axis_index("fsdp")
    me = lax.axis_index("seq")
    rows = w_ref.shape[0]
    quarter = rows // 4
    local = x_ref.shape[0]
    gw = c_all.shape[1]
    greet(seq_count, fsdp_count, dp)

    def part(block, q):
        return w_all.at[pl.ds(pl.multiple_of(block * rows + q * quarter, 16), quarter)]

    def remote(src, dst, send, recv, where):
        return pltpu.make_async_remote_copy(
            src_ref=src, dst_ref=dst, send_sem=send, recv_sem=recv, device_id=where, device_id_type=MESH
        )

    sent = []
    z_copies = {}
    for d in range(1, fsdp_count):
        copy = remote(
            w_ref.at[pl.ds(pl.multiple_of(dp * quarter, 16), quarter)],
            part(fs, dp), zs.at[d], zr.at[d], {"fsdp": ring("fsdp", d)},
        )
        copy.start()
        z_copies[d] = copy
        sent.append(copy)
    here = pl.ds(pl.multiple_of(me * local, 16), local)
    seq_copies = []
    for d in range(1, seq_count):
        peer = ring("seq", d)
        a = remote(x_ref, x_all.at[here], xs.at[d], xr.at[d], {"seq": peer})
        b = remote(
            c_ref.at[:, pl.ds(pl.multiple_of(peer * gw, 128), gw)],
            c_all.at[here], cs.at[d], cr.at[d], {"seq": peer},
        )
        a.start()
        b.start()
        seq_copies += [a, b]
    mine = [
        pltpu.make_async_copy(w_ref, w_all.at[pl.ds(pl.multiple_of(fs * rows, 16), rows)], local_sem.at[0]),
        pltpu.make_async_copy(x_ref, x_all.at[here], local_sem.at[1]),
        pltpu.make_async_copy(
            c_ref.at[:, pl.ds(pl.multiple_of(me * gw, 128), gw)], c_all.at[here], local_sem.at[2]
        ),
    ]
    for copy in mine:
        copy.start()
    order = sorted(range(1, fsdp_count), key=lambda d: min(d, fsdp_count - d))
    first, second, third = {}, {}, {}
    for d in order:
        z_copies[d].wait_recv()
        block = ring("fsdp", -d)
        second[d] = remote(part(block, dp), part(block, dp), f2s.at[d], f2r.at[d], {"dp": dp ^ 2})
        second[d].start()
        first[d] = remote(part(block, dp), part(block, dp), f1s.at[d], f1r.at[d], {"dp": dp ^ 1})
        first[d].start()
    for d in order:
        second[d].wait_recv()
        block = ring("fsdp", -d)
        third[d] = remote(part(block, dp ^ 2), part(block, dp ^ 2), f3s.at[d], f3r.at[d], {"dp": dp ^ 1})
        third[d].start()
    for d in order:
        first[d].wait_recv()
        third[d].wait_recv()
    for copy in seq_copies:
        copy.wait_recv()
    for copy in mine:
        copy.wait()
    for copy in sent + seq_copies:
        copy.wait_send()
    for d in order:
        first[d].wait_send()
        second[d].wait_send()
        third[d].wait_send()


def gather(w_mine, x, c, seq_count, fsdp_count, gw):
    any_spec = pl.BlockSpec(memory_space=pl.ANY)
    dma = pltpu.SemaphoreType.DMA
    total = x.shape[0] * seq_count
    return pl.pallas_call(
        functools.partial(gather_kernel, seq_count, fsdp_count),
        out_shape=(
            jax.ShapeDtypeStruct((w_mine.shape[0] * fsdp_count, w_mine.shape[1]), BF16),
            jax.ShapeDtypeStruct((total, x.shape[1]), BF16),
            jax.ShapeDtypeStruct((total, gw), BF16),
        ),
        in_specs=[any_spec] * 3,
        out_specs=(any_spec,) * 3,
        scratch_shapes=[dma((3,))] + [dma((seq_count,))] * 4 + [dma((fsdp_count,))] * 8,
        compiler_params=pltpu.CompilerParams(collective_id=0, has_side_effects=True),
        name="gather_inputs",
    )(w_mine, x, c)


def nt(a, b):
    return lax.dot_general(a, b, (((1,), (1,)), ((), ())), preferred_element_type=F32)


def tn(a, b):
    return lax.dot_general(a, b, (((0,), (0,)), ((), ())), preferred_element_type=F32)


def attention_kernel(len_ref, q_ref, k_ref, v_ref, o_ref, ctx_ref, grad_ref, dk_acc, dv_acc):
    pair = pl.program_id(0)
    step = pl.program_id(1)
    steps = pl.num_programs(1)
    length = len_ref[0]
    block, width = q_ref.shape
    keys = k_ref.shape[0]
    gw = grad_ref.shape[1] // 3
    factor = 1.0 / math.sqrt(HD)
    key_ok = lax.broadcasted_iota(jnp.int32, (keys, block), 0) < length
    row = lax.broadcasted_iota(jnp.int32, (block, width), 0) + step * block
    row_ok = row < length
    k, v, q = k_ref[...], v_ref[...], q_ref[...]
    upstream = jnp.where(row_ok, o_ref[...], jnp.zeros_like(o_ref[...]))
    key_lane = lax.broadcasted_iota(jnp.int32, (keys, width), 1)
    row_lane = lax.broadcasted_iota(jnp.int32, (block, width), 1)

    @pl.when(step == 0)
    def _():
        dk_acc[...] = jnp.zeros_like(dk_acc)
        dv_acc[...] = jnp.zeros_like(dv_acc)

    context_t = jnp.zeros((width, block), F32)
    query_t = jnp.zeros((width, block), F32)
    dk = dk_acc[...]
    dv = dv_acc[...]
    for head in range(width // HD):
        low, high = head * HD, (head + 1) * HD
        on_key = (key_lane >= low) & (key_lane < high)
        on_row = (row_lane >= low) & (row_lane < high)
        k_h = jnp.where(on_key, k, jnp.zeros_like(k))
        v_h = jnp.where(on_key, v, jnp.zeros_like(v))
        q_h = jnp.where(on_row, q, jnp.zeros_like(q))
        o_h = jnp.where(on_row, upstream, jnp.zeros_like(upstream))
        scores = jnp.where(key_ok, nt(k_h, q), -jnp.inf)
        peak = jnp.max(scores, axis=0, keepdims=True)
        e = jnp.exp((scores - peak) * factor)
        p = e * (1.0 / jnp.sum(e, axis=0, keepdims=True))
        weights = p.astype(BF16)
        context_t += tn(v_h, weights)
        dv += jnp.dot(weights, o_h, preferred_element_type=F32)
        dp = nt(v_h, upstream)
        inner = jnp.sum(p * dp, axis=0, keepdims=True)
        ds = (p * (dp - inner) * factor).astype(BF16)
        query_t += tn(k_h, ds)
        dk += jnp.dot(ds, q_h, preferred_element_type=F32)
    context = context_t.T
    ctx_ref[...] = jnp.where(row_ok, context, jnp.zeros_like(context)).astype(BF16)
    rows = pl.ds(pl.multiple_of(step * block, block), block)
    column = pl.multiple_of(pair * width, width)
    grad_ref[rows, pl.ds(column, width)] = query_t.T.astype(BF16)
    dk_acc[...] = dk
    dv_acc[...] = dv

    @pl.when(step == steps - 1)
    def _():
        grad_ref[:, pl.ds(pl.multiple_of(gw + column, width), width)] = dk.astype(BF16)
        grad_ref[:, pl.ds(pl.multiple_of(2 * gw + column, width), width)] = dv.astype(BF16)


def attention(length, packed, c_all, gw):
    total = packed.shape[0]
    block = min(total, 512)
    width = 2 * HD
    pairs = gw // width
    return pl.pallas_call(
        attention_kernel,
        grid=(pairs, total // block),
        out_shape=(
            jax.ShapeDtypeStruct((total, gw), BF16),
            jax.ShapeDtypeStruct((total, 3 * gw), BF16),
        ),
        in_specs=[
            pl.BlockSpec(memory_space=pltpu.SMEM),
            pl.BlockSpec((block, width), lambda h, i: (i, h)),
            pl.BlockSpec((total, width), lambda h, i: (0, pairs + h)),
            pl.BlockSpec((total, width), lambda h, i: (0, 2 * pairs + h)),
            pl.BlockSpec((block, width), lambda h, i: (i, h)),
        ],
        out_specs=(
            pl.BlockSpec((block, width), lambda h, i: (i, h)),
            pl.BlockSpec((total, 3 * gw), lambda h, i: (0, 0)),
        ),
        scratch_shapes=[pltpu.VMEM((total, width), F32)] * 2,
        compiler_params=pltpu.CompilerParams(vmem_limit_bytes=VMEM_BYTES),
        cost_estimate=pl.CostEstimate(
            flops=12 * total * total * gw, bytes_accessed=16 * total * gw, transcendentals=total * total * gw // HD
        ),
        name="attention",
    )(length, packed, packed, packed, c_all)


def encode(value):
    peak = jnp.maximum(jnp.max(jnp.abs(value), axis=0, keepdims=True), 1e-30)
    code = jnp.round(value * (32767.0 / peak)).astype(jnp.int32).astype(jnp.int16)
    return code, peak * (1.0 / 32767.0)


def decode(code, scale):
    return code.astype(jnp.int32).astype(F32) * scale


def reduce_kernel(
    seq_count, fsdp_count, nt_ref, grad_ref, dx_ref, ctx_ref, out_ref, dx_out, ctx_out,
    s1, r1, s2, r2, t2, u2, s3, r3, t3, u3, total, s4,
    local_sem, s1s, s1r, s2s, s2r, t2s, t2r, s3s, s3r, t3s, t3r, s4s, s4r, xs, xr, cs, cr,
):
    dp = lax.axis_index("dp")
    fs = lax.axis_index("fsdp")
    me = lax.axis_index("seq")
    features = nt_ref.shape[0]
    rows = features // (4 * fsdp_count)
    local = dx_out.shape[1]
    gw = ctx_ref.shape[1]
    final = rows // seq_count
    greet(seq_count, fsdp_count, dp)

    def remote(src, dst, send, recv, where):
        return pltpu.make_async_remote_copy(
            src_ref=src, dst_ref=dst, send_sem=send, recv_sem=recv, device_id=where, device_id_type=MESH
        )

    mine_columns = pl.ds(pl.multiple_of(me * gw, 128), gw)
    seq_copies = []
    for d in range(1, seq_count):
        peer = ring("seq", d)
        there = pl.ds(pl.multiple_of(peer * local, 16), local)
        a = remote(dx_ref.at[there], dx_out.at[d - 1], xs.at[d], xr.at[d], {"seq": peer})
        b = remote(ctx_ref.at[there], ctx_out.at[:, mine_columns], cs.at[d], cr.at[d], {"seq": peer})
        seq_copies += [a, b]
    own = pltpu.make_async_copy(
        ctx_ref.at[pl.ds(pl.multiple_of(me * local, 16), local)], ctx_out.at[:, mine_columns], local_sem
    )
    for copy in seq_copies:
        copy.start()
    own.start()

    def product(block, step):
        sub = lax.rem(fs + 1 + step, fsdp_count)
        start = pl.multiple_of(block * (rows * fsdp_count) + sub * rows, 16)
        return jnp.dot(nt_ref[pl.ds(start, rows), :], grad_ref[...], preferred_element_type=F32)

    core = lax.rem(dp, 2)
    far = 2 * (1 - dp // 2)
    near = 2 * (dp // 2)

    def copy1(i):
        return remote(s1.at[i], r1.at[i], s1s.at[i], s1r.at[i], {"dp": dp ^ 1})

    def copy2(d):
        return (
            remote(s2.at[d], r2.at[d], s2s.at[d], s2r.at[d], {"dp": dp ^ 2}),
            remote(t2.at[d], u2.at[d], t2s.at[d], t2r.at[d], {"dp": dp ^ 2}),
        )

    def copy3(d):
        peer = lax.rem(fs + 1 + d, fsdp_count)
        return (
            remote(s3.at[d], r3.at[d], s3s.at[d], s3r.at[d], {"fsdp": peer}),
            remote(t3.at[d], u3.at[d], t3s.at[d], t3r.at[d], {"fsdp": peer}),
        )

    def loop(count, body):
        lax.fori_loop(0, count, lambda i, _: (body(i), 0)[1], 0)

    def to_core(i):
        block = jnp.where(i < fsdp_count, far, near) + (1 - core)
        s1[i] = product(block, lax.rem(i, fsdp_count))
        copy1(i).start()

    loop(2 * fsdp_count, to_core)

    def to_x(d):
        own_part = product(far + core, d)
        copy1(d).wait_recv()
        code, scale = encode(own_part + r1[d])
        s2[d] = code
        t2[d] = scale
        for copy in copy2(d):
            copy.start()

    loop(fsdp_count, to_x)

    def arrived(d):
        own_part = product(near + core, d)
        copy1(fsdp_count + d).wait_recv()
        for copy in copy2(d):
            copy.wait_recv()
        return own_part + r1[fsdp_count + d] + decode(r2[d], u2[d])

    def to_z(d):
        code, scale = encode(arrived(d))
        s3[d] = code
        t3[d] = scale
        for copy in copy3(d):
            copy.start()

    loop(fsdp_count - 1, to_z)
    total[...] = arrived(fsdp_count - 1)

    def add_z(d):
        for copy in copy3(d):
            copy.wait_recv()
        total[...] += decode(r3[d], u3[d])

    loop(fsdp_count - 1, add_z)
    for p in range(seq_count):
        s4[p] = total[p * final : (p + 1) * final, :]
    last = []
    for d in range(1, seq_count):
        peer = ring("seq", d)
        copy = remote(s4.at[peer], out_ref.at[me], s4s.at[d], s4r.at[d], {"seq": peer})
        copy.start()
        last.append(copy)
    out_ref[me] = s4[me]
    for copy in last:
        copy.wait()
    for copy in seq_copies:
        copy.wait()
    own.wait()

    def drain1(i):
        copy1(i).wait_send()

    def drain2(d):
        for copy in copy2(d):
            copy.wait_send()

    def drain3(d):
        for copy in copy3(d):
            copy.wait_send()

    loop(2 * fsdp_count, drain1)
    loop(fsdp_count, drain2)
    loop(fsdp_count - 1, drain3)


def reduce(normed_t, grad, dx, ctx, seq_count, fsdp_count, local):
    features, columns = normed_t.shape[0], grad.shape[1]
    gw = columns // 3
    rows = features // (4 * fsdp_count)
    final = rows // seq_count
    vmem = pl.BlockSpec(memory_space=pltpu.VMEM)
    any_spec = pl.BlockSpec(memory_space=pl.ANY)
    dma = pltpu.SemaphoreType.DMA
    n = fsdp_count
    i16 = jnp.int16
    return pl.pallas_call(
        functools.partial(reduce_kernel, seq_count, fsdp_count),
        out_shape=(
            jax.ShapeDtypeStruct((seq_count, final, columns), F32),
            jax.ShapeDtypeStruct((max(seq_count - 1, 1), local, features), BF16),
            jax.ShapeDtypeStruct((local, seq_count * gw), BF16),
        ),
        in_specs=[vmem, vmem, any_spec, any_spec],
        out_specs=(vmem, any_spec, any_spec),
        scratch_shapes=[
            pltpu.VMEM((2 * n, rows, columns), F32),
            pltpu.VMEM((2 * n, rows, columns), F32),
            pltpu.VMEM((n, rows, columns), i16),
            pltpu.VMEM((n, rows, columns), i16),
            pltpu.VMEM((n, 1, columns), F32),
            pltpu.VMEM((n, 1, columns), F32),
            pltpu.VMEM((n, rows, columns), i16),
            pltpu.VMEM((n, rows, columns), i16),
            pltpu.VMEM((n, 1, columns), F32),
            pltpu.VMEM((n, 1, columns), F32),
            pltpu.VMEM((rows, columns), F32),
            pltpu.VMEM((seq_count, final, columns), F32),
            dma,
        ]
        + [dma((2 * n,))] * 2
        + [dma((n,))] * 8
        + [dma((seq_count,))] * 6,
        compiler_params=pltpu.CompilerParams(
            collective_id=1, has_side_effects=True, vmem_limit_bytes=VMEM_BYTES
        ),
        name="reduce_gradients",
    )(normed_t, grad, dx, ctx)


def standardise(rows):
    as_float = rows.astype(F32)
    centered = as_float - jnp.mean(as_float, axis=1, keepdims=True)
    inv_std = lax.rsqrt(jnp.mean(centered * centered, axis=1, keepdims=True) + EPS)
    return centered * inv_std, inv_std


def body(frames, projection, lengths, cotangent):
    inputs = frames[0]
    upstream = cotangent[0]
    seq_count = lax.axis_size("seq")
    fsdp_count = lax.axis_size("fsdp")
    me = lax.axis_index("seq")
    local, features = inputs.shape
    gw = HEADS // seq_count * HD
    w_mine = lax.dynamic_index_in_dim(
        projection.reshape(-1, 3, seq_count, gw), me, axis=2, keepdims=False
    ).reshape(-1, 3 * gw)
    w_all, x_all, c_all = gather(w_mine, inputs, upstream, seq_count, fsdp_count, gw)
    normed = standardise(x_all)[0].astype(BF16)
    packed = jnp.dot(normed, w_all, preferred_element_type=F32).astype(BF16)
    ctx, grad = attention(lengths, packed, c_all, gw)
    partial = nt(grad, w_all)
    out, dx, context = reduce(
        normed.T, grad, partial.astype(BF16), ctx, seq_count, fsdp_count, local
    )
    normed_gradient = lax.dynamic_slice_in_dim(partial, me * local, local, 0)
    for d in range(seq_count - 1):
        normed_gradient = normed_gradient + dx[d].astype(F32)
    standard, inv_std = standardise(inputs)
    row_mean = jnp.mean(normed_gradient, axis=1, keepdims=True)
    projected = jnp.mean(normed_gradient * standard, axis=1, keepdims=True)
    input_gradient = inv_std * (normed_gradient - row_mean - standard * projected)
    projection_gradient = (
        out.reshape(seq_count, -1, 3, gw).transpose(1, 2, 0, 3).reshape(-1, 3 * seq_count * gw)
    )
    return (context[None], input_gradient[None], projection_gradient)


def solution(mesh):
    placed = (
        P(("dp", "fsdp"), "seq", None),
        P("fsdp", None),
        P(("dp", "fsdp")),
        P(("dp", "fsdp"), "seq", None),
    )
    return jax.shard_map(
        body,
        mesh=mesh,
        in_specs=placed,
        out_specs=(
            P(("dp", "fsdp"), "seq", None),
            P(("dp", "fsdp"), "seq", None),
            P(("dp", "fsdp", "seq"), None),
        ),
        check_vma=False,
    )
```

time: 523 us -> 166 us (0.32)
  waiting for transfers between devices: 358 us -> 0 us
  Pallas kernels: 0 us -> 136 us
  matrix products: 67.1 us -> 9.54 us
  blocking collectives: 36.7 us -> 0 us
  local copies, waits for them, and re-layouts: 29.1 us -> 10.4 us
  between operations: 14.9 us -> 1.38 us
  starting transfers between devices: 8.17 us -> 0 us
    reduce_scatter x1 -> x0, waiting for transfers between devices: 175 us -> none  [body(): lax.psum_scatter(lax.dot_general(normed, packed_gradient, (((0,), (0,)),...]
    all_gather x1 -> x0, waiting for transfers between devices: 164 us -> none  [body(): weight_full = lax.all_gather(projection, 'fsdp', axis=0, tiled=True)]
    pallas_call x0 -> x3, Pallas kernels: none -> 136 us  [the longest x1 74.1 us: gather(): pl.pallas_call(functools.partial(gather_kernel, seq_count, fsdp_count), o...]
    dot_general x8 -> x2, matrix products: 61.8 us -> 9.54 us  [the longest x1 5.79 us: nt(): lax.dot_general(a, b, (((1,), (1,)), ((), ())), preferred_element_type=F32)]
    all_to_all x2 -> x0, blocking collectives: 36.7 us -> none  [the longest x1 27 us: body(): lax.all_to_all(stacked, 'seq', split_axis=0, concat_axis=2, tiled=True)]
    all_to_all x2 -> x0, waiting for transfers between devices: 18 us -> none  [the longest x1 18 us: body(): lax.all_to_all(packed, 'seq', split_axis=2, concat_axis=0, tiled=True)]
    all_to_all x2 -> x0, starting transfers between devices: 7.91 us -> none  [the longest x1 4.23 us: body(): lax.all_to_all(upstream_four, 'seq', split_axis=2, concat_axis=0, tiled=T...]
    all_to_all x5 -> x0, local copies, waits for them, and re-layouts: 7.82 us -> none  [the longest x2 3.24 us: body(): lax.all_to_all(stacked, 'seq', split_axis=0, concat_axis=2, tiled=True)]
  transfers between devices with their start and end apart: 4 -> 0, of which waited for: 3 -> 0; matrix products, arithmetic and copies ran while one was open for 7% -> 0% of each run, Pallas kernels for 0% -> 0%
where the time goes in v1:
time: 166 us; the launch traced here: 164 us
  Pallas kernels  136 us (82%)
  local copies, waits for them, and re-layouts  10.4 us (6%)
  matrix products  9.54 us (6%)
  other arithmetic  6.63 us (4%)
    pallas_call x1, Pallas kernels, gather(): pl.pallas_call(functools.partial(gather_kernel, seq_count, fsdp_count), o...  74.1 us
    pallas_call x1, Pallas kernels, reduce(): pl.pallas_call(functools.partial(reduce_kernel, seq_count, fsdp_count), o...  49.6 us
    pallas_call x1, Pallas kernels, attention(): pl.pallas_call(attention_kernel, grid=(pairs, total // block), out_shape=...  12.5 us
    dot_general x1, matrix products, nt(): lax.dot_general(a, b, (((1,), (1,)), ((), ())), preferred_element_type=F32)  5.79 us
    unnamed x14, local copies, waits for them, and re-layouts  4.89 us
    dot_general x1, matrix products, body(): packed = jnp.dot(normed, w_all, preferred_element_type=F32).astype(BF16)  3.74 us

profile of v1, /device:TPU:0, one launch (start us, length us, event | category | flops | bytes accessed | tf_op | source)
XLA Modules:
  0.0 164.0 jit_solution(17963566583473028975)
XLA Ops:
  0.6 3.0 %copy.12 = bf16[384,3072]{0,1:T(8,128)(2,1)S(1)} copy(bf16[384,3072]{1,0:T(8,128)(2,1)} %param.5) | data formatting | bytes 4718592 | tf_op args[1]
  3.6 0.1 constant_dynamic-slice_fusion
  3.8 1.5 copy.13.w_ref
  5.2 74.1 %gather_inputs.1 = (bf16[1536,1536]{1,0:T(8,128)(2,1)}, bf16[512,1536]{1,0:T(8,128)(2,1)}, bf16[512,512]{1,0:T(8,128)(2,1)}) custom-call(bf16[384,1536]{1,0:T(8,128)(2,1)} %copy.13.w_ref, bf16[256,1536]{1,0:T(8,128)(2,1)} %bitcast.26, bf16[256,1024]{1,0:T(8,128)(2,1)} %bitcast.30), custom_call_target="tpu_custom_call" | custom-call | tf_op jit(solution)/shard_map/gather_inputs/pallas_call | solution.py:121
  79.3 1.7 %copy.14 = bf16[512,1536]{0,1:T(8,128)(2,1)S(1)} copy(bf16[512,1536]{1,0:T(8,128)(2,1)} %get-tuple-element.11) | data formatting | bytes 3145728 | tf_op jit(solution)/shard_map/gather_inputs/pallas_call | solution.py:121
  81.0 0.3 convert_reduce_fusion
  81.3 0.0 copy-start.5
  81.3 0.5 fusion.2
  81.8 1.5 fusion.14.nt_ref
  84.0 0.2 copy-done.5
  84.2 3.7 %convolution_convert_fusion.q_ref.k_ref.v_ref = bf16[512,1536]{1,0:T(8,128)(2,1)} fusion(bf16[1536,1536]{1,0:T(8,128)(2,1)S(1)} %copy-done.5, bf16[512,1536]{0,1:T(8,128)(2,1)S(1)} %copy.14, f32[512]{0:T(512)S(1)} %add_rsqrt_fusion, f32[512]{0:T(512)S(1)} %broadcast_multiply_fusion), kind=kOutput, calls=%fused_computation.6 | convolution fusion | flops 2419851264 | bytes 7868416 | tf_op jit(solution)/shard_map/dot_general | solution.py:445
  88.0 12.5 %attention.1 = (bf16[512,512]{1,0:T(8,128)(2,1)}, bf16[512,1536]{1,0:T(8,128)(2,1)}) custom-call(s32[1]{0:T(128)S(6)} %copy.17.len_ref, bf16[512,1536]{1,0:T(8,128)(2,1)} %convolution_convert_fusion.q_ref.k_ref.v_ref, bf16[512,1536]{1,0:T(8,128)(2,1)} %convolution_convert_fusion.q_ref.k_ref.v_ref, ...), custom_call_target="tpu_custom_call" | custom-call | flops 1610612736 | bytes 4194304 | tf_op jit(solution)/shard_map/attention/pallas_call | solution.py:209
  100.4 5.8 %fusion.16 = (bf16[512,1536]{1,0:T(8,128)(2,1)}, f32[512,1536]{1,0:T(8,128)}) fusion(bf16[512,1536]{1,0:T(8,128)(2,1)} %get-tuple-element.14.grad_ref, bf16[1536,1536]{1,0:T(8,128)(2,1)S(1)} %copy-done.5), kind=kOutput, calls=%fused_computation.28 | convolution fusion | flops 2416705536 | bytes 11010048 | tf_op jit(solution)/shard_map/dot_general | solution.py:137
  106.2 0.0 copy-start
  106.2 49.6 %reduce_gradients.1 = (f32[2,48,1536]{2,1,0:T(8,128)}, bf16[1,256,1536]{2,1,0:T(8,128)(2,1)}, bf16[256,1024]{1,0:T(8,128)(2,1)}) custom-call(bf16[1536,512]{1,0:T(8,128)(2,1)} %fusion.14.nt_ref, bf16[512,1536]{1,0:T(8,128)(2,1)} %get-tuple-element.14.grad_ref, bf16[512,1536]{1,0:T(8,128)(2,1)} %get-tuple-element.21.dx_ref, ...), custom_call_target="tpu_custom_call" | custom-call | tf_op jit(solution)/shard_map/reduce_gradients/pallas_call | solution.py:391
  155.8 0.0 copy-start.2
  155.8 0.0 copy-done
  155.8 0.2 convert_reduce_fusion.1
  156.0 0.3 fusion.12
  156.4 0.6 copy-done.2
  156.9 0.0 copy-start.1
  156.9 2.1 %fusion.15 = (f32[256]{0:T(256)S(1)}, f32[256]{0:T(256)S(1)}) fusion(bf16[1,256,1536]{2,1,0:T(8,128)(2,1)S(1)} %copy-done.2, f32[512,1536]{1,0:T(8,128)} %get-tuple-element.22, s32[]{:T(128)S(6)} %select_n.8, f32[256]{0:T(256)S(1)} %add_rsqrt_fusion.1, f32[256]{0:T(256)S(1)} %broadcast_multiply_fusion.3, bf16[1,256,1536]{2,1,0:T(8,128)(2,1)S(1)} %copy-done), kind=kLoop, calls=%fused_computation.20 | loop fusion | flops 3145216 | bytes 3149828 | tf_op jit(solution)/shard_map/reduce_sum | solution.py:455
  159.0 0.3 copy-done.1
  159.3 0.0 copy-start.3
  159.3 1.7 %fusion.11 = f32[1,256,1536]{2,1,0:T(8,128)} fusion(f32[256]{0:T(256)S(1)} %get-tuple-element.23, f32[256]{0:T(256)S(1)} %get-tuple-element.24, f32[256]{0:T(256)S(1)} %add_rsqrt_fusion.1, f32[256]{0:T(256)S(1)} %broadcast_multiply_fusion.3, bf16[1,256,1536]{2,1,0:T(8,128)(2,1)S(1)} %copy-done.2, f32[512,1536]{1,0:T(8,128)S(1)} %copy-done.1, ...), kind=kLoop, calls=%fused_computation.16 | loop fusion | flops 3538944 | bytes 4722692 | tf_op jit(solution)/shard_map/broadcast_in_dim | solution.py:461
  161.0 0.0 copy-done.3
  161.0 0.4 reshape.55
  161.5 0.0 copy-start.4
  161.5 0.5 copy.15
  161.9 1.3 reshape.56
  163.2 0.0 copy-done.4
  163.3 0.8 copy.18
  (5 shorter events, 0.0 us)
Async XLA Ops:
  81.3 2.9 %copy-start.5 = (bf16[1536,1536]{1,0:T(8,128)(2,1)S(1)}, bf16[1536,1536]{1,0:T(8,128)(2,1)}, u32[]{:S(2)}) copy-start(bf16[1536,1536]{1,0:T(8,128)(2,1)} %get-tuple-element.12) | copy-start | bytes 14155780
  106.2 49.6 %copy-start = (bf16[1,256,1536]{2,1,0:T(8,128)(2,1)S(1)}, bf16[1,256,1536]{2,1,0:T(8,128)(2,1)}, u32[]{:S(2)}) copy-start(bf16[1,256,1536]{2,1,0:T(8,128)(2,1)} %param.4) | copy-start | bytes 2359300
  155.8 1.1 copy-start.2
  156.9 2.4 %copy-start.1 = (f32[512,1536]{1,0:T(8,128)S(1)}, f32[512,1536]{1,0:T(8,128)}, u32[]{:S(2)}) copy-start(f32[512,1536]{1,0:T(8,128)} %get-tuple-element.22) | copy-start | bytes 9437188
  159.3 1.7 %copy-start.3 = (f32[2,48,1536]{2,1,0:T(8,128)S(1)}, f32[2,48,1536]{2,1,0:T(8,128)}, u32[]{:S(2)}) copy-start(f32[2,48,1536]{2,1,0:T(8,128)} %get-tuple-element.18) | copy-start | bytes 1769476
  161.5 1.8 %copy-start.4 = (bf16[256,1024]{1,0:T(8,128)(2,1)S(1)}, bf16[256,1024]{1,0:T(8,128)(2,1)}, u32[]{:S(2)}) copy-start(bf16[256,1024]{1,0:T(8,128)(2,1)} %get-tuple-element.16) | copy-start | bytes 1572868

commit v2 on v1

--- a/solution.py
+++ b/solution.py
@@ -34,7 +34,7 @@
 
 
 def gather_kernel(
-    seq_count, fsdp_count, w_ref, x_ref, c_ref, w_all, x_all, c_all,
+    seq_count, n, w_ref, x_ref, c_ref, w_all, x_all, c_all,
     local_sem, xs, xr, cs, cr, zs, zr, f1s, f1r, f2s, f2r, f3s, f3r,
 ):
     dp = lax.axis_index("dp")
@@ -44,7 +44,20 @@
     quarter = rows // 4
     local = x_ref.shape[0]
     gw = c_all.shape[1]
-    greet(seq_count, fsdp_count, dp)
+    block_rows = pl.ds(pl.multiple_of(fs * rows, 16), rows)
+    picks = []
+    for kind in range(3):
+        column = pl.multiple_of((kind * seq_count + me) * gw, 128)
+        picks.append(
+            pltpu.make_async_copy(
+                w_ref.at[:, pl.ds(column, gw)],
+                w_all.at[block_rows, pl.ds(kind * gw, gw)],
+                local_sem.at[kind],
+            )
+        )
+    for copy in picks:
+        copy.start()
+    greet(seq_count, n, dp)
 
     def part(block, q):
         return w_all.at[pl.ds(pl.multiple_of(block * rows + q * quarter, 16), quarter)]
@@ -54,16 +67,31 @@
             src_ref=src, dst_ref=dst, send_sem=send, recv_sem=recv, device_id=where, device_id_type=MESH
         )
 
-    sent = []
-    z_copies = {}
-    for d in range(1, fsdp_count):
-        copy = remote(
-            w_ref.at[pl.ds(pl.multiple_of(dp * quarter, 16), quarter)],
-            part(fs, dp), zs.at[d], zr.at[d], {"fsdp": ring("fsdp", d)},
-        )
-        copy.start()
-        z_copies[d] = copy
-        sent.append(copy)
+    def along(block, index, up):
+        peer = ring("fsdp", 1 if up else -1)
+        return remote(part(block, dp), part(block, dp), zs.at[index], zr.at[index], {"fsdp": peer})
+
+    def forward1(block, index):
+        return remote(part(block, dp), part(block, dp), f1s.at[index], f1r.at[index], {"dp": dp ^ 1})
+
+    def forward2(block, index):
+        return remote(part(block, dp), part(block, dp), f2s.at[index], f2r.at[index], {"dp": dp ^ 2})
+
+    def forward3(block, index):
+        other = part(block, dp ^ 2)
+        return remote(other, other, f3s.at[index], f3r.at[index], {"dp": dp ^ 1})
+
+    for copy in picks:
+        copy.wait()
+
+    @pl.when(fs < n - 1)
+    def _():
+        along(fs, 1, True).start()
+
+    @pl.when(fs > 0)
+    def _():
+        along(fs, n + 1, False).start()
+
     here = pl.ds(pl.multiple_of(me * local, 16), local)
     seq_copies = []
     for d in range(1, seq_count):
@@ -76,61 +104,86 @@
         a.start()
         b.start()
         seq_copies += [a, b]
-    mine = [
-        pltpu.make_async_copy(w_ref, w_all.at[pl.ds(pl.multiple_of(fs * rows, 16), rows)], local_sem.at[0]),
-        pltpu.make_async_copy(x_ref, x_all.at[here], local_sem.at[1]),
-        pltpu.make_async_copy(
-            c_ref.at[:, pl.ds(pl.multiple_of(me * gw, 128), gw)], c_all.at[here], local_sem.at[2]
-        ),
-    ]
-    for copy in mine:
-        copy.start()
-    order = sorted(range(1, fsdp_count), key=lambda d: min(d, fsdp_count - d))
-    first, second, third = {}, {}, {}
-    for d in order:
-        z_copies[d].wait_recv()
-        block = ring("fsdp", -d)
-        second[d] = remote(part(block, dp), part(block, dp), f2s.at[d], f2r.at[d], {"dp": dp ^ 2})
-        second[d].start()
-        first[d] = remote(part(block, dp), part(block, dp), f1s.at[d], f1r.at[d], {"dp": dp ^ 1})
-        first[d].start()
-    for d in order:
-        second[d].wait_recv()
-        block = ring("fsdp", -d)
-        third[d] = remote(part(block, dp ^ 2), part(block, dp ^ 2), f3s.at[d], f3r.at[d], {"dp": dp ^ 1})
-        third[d].start()
-    for d in order:
-        first[d].wait_recv()
-        third[d].wait_recv()
+    x_all[here, :] = x_ref[...]
+    c_all[here, :] = c_ref[:, pl.ds(pl.multiple_of(me * gw, 128), gw)]
+
+    def each(act):
+        for t in range(1, n):
+            for up in (True, False):
+                block = fs - t if up else fs + t
+                exists = (block >= 0) & (block <= n - 1)
+                index = t if up else n + t
+
+                @pl.when(exists)
+                def _():
+                    act(block, index, up)
+
+    def goes_on(up):
+        return fs < n - 1 if up else fs > 0
+
+    def take(block, index, up):
+        along(block, index, up).wait_recv()
+
+        @pl.when(goes_on(up))
+        def _():
+            along(block, index + 1, up).start()
+
+        forward2(block, index).start()
+        forward1(block, index).start()
+
+    def pass_on(block, index, up):
+        forward2(block, index).wait_recv()
+        forward3(block, index).start()
+
+    def finish(block, index, up):
+        forward1(block, index).wait_recv()
+        forward3(block, index).wait_recv()
+
+    def drain(block, index, up):
+        @pl.when(goes_on(up))
+        def _():
+            along(block, index + 1, up).wait_send()
+
+        forward1(block, index).wait_send()
+        forward2(block, index).wait_send()
+        forward3(block, index).wait_send()
+
+    each(take)
+    each(pass_on)
+    each(finish)
     for copy in seq_copies:
-        copy.wait_recv()
-    for copy in mine:
         copy.wait()
-    for copy in sent + seq_copies:
-        copy.wait_send()
-    for d in order:
-        first[d].wait_send()
-        second[d].wait_send()
-        third[d].wait_send()
-
-
-def gather(w_mine, x, c, seq_count, fsdp_count, gw):
+    each(drain)
+
+    @pl.when(fs < n - 1)
+    def _():
+        along(fs, 1, True).wait_send()
+
+    @pl.when(fs > 0)
+    def _():
+        along(fs, n + 1, False).wait_send()
+
+
+def gather(w, x, c, seq_count, fsdp_count, gw):
     any_spec = pl.BlockSpec(memory_space=pl.ANY)
+    vmem = pl.BlockSpec(memory_space=pltpu.VMEM)
     dma = pltpu.SemaphoreType.DMA
     total = x.shape[0] * seq_count
     return pl.pallas_call(
         functools.partial(gather_kernel, seq_count, fsdp_count),
         out_shape=(
-            jax.ShapeDtypeStruct((w_mine.shape[0] * fsdp_count, w_mine.shape[1]), BF16),
+            jax.ShapeDtypeStruct((w.shape[0] * fsdp_count, 3 * gw), BF16),
             jax.ShapeDtypeStruct((total, x.shape[1]), BF16),
             jax.ShapeDtypeStruct((total, gw), BF16),
         ),
-        in_specs=[any_spec] * 3,
-        out_specs=(any_spec,) * 3,
-        scratch_shapes=[dma((3,))] + [dma((seq_count,))] * 4 + [dma((fsdp_count,))] * 8,
-        compiler_params=pltpu.CompilerParams(collective_id=0, has_side_effects=True),
+        in_specs=[any_spec, vmem, vmem],
+        out_specs=(vmem,) * 3,
+        scratch_shapes=[dma((3,))] + [dma((seq_count,))] * 4 + [dma((2 * fsdp_count + 1,))] * 8,
+        compiler_params=pltpu.CompilerParams(
+            collective_id=0, has_side_effects=True, vmem_limit_bytes=VMEM_BYTES
+        ),
         name="gather_inputs",
-    )(w_mine, x, c)
+    )(w, x, c)
 
 
 def nt(a, b):
@@ -244,8 +297,8 @@
 
 
 def reduce_kernel(
-    seq_count, fsdp_count, nt_ref, grad_ref, dx_ref, ctx_ref, out_ref, dx_out, ctx_out,
-    s1, r1, s2, r2, t2, u2, s3, r3, t3, u3, total, s4,
+    seq_count, fsdp_count, nt_ref, grad_ref, w_ref, frames_ref, ctx_ref, out_ref, input_out, ctx_out,
+    s1, r1, s2, r2, t2, u2, s3, r3, t3, u3, total, s4, r4, sdx, rdx, normed_gradient,
     local_sem, s1s, s1r, s2s, s2r, t2s, t2r, s3s, s3r, t3s, t3r, s4s, s4r, xs, xr, cs, cr,
 ):
     dp = lax.axis_index("dp")
@@ -253,7 +306,7 @@
     me = lax.axis_index("seq")
     features = nt_ref.shape[0]
     rows = features // (4 * fsdp_count)
-    local = dx_out.shape[1]
+    local = frames_ref.shape[0]
     gw = ctx_ref.shape[1]
     final = rows // seq_count
     greet(seq_count, fsdp_count, dp)
@@ -268,9 +321,8 @@
     for d in range(1, seq_count):
         peer = ring("seq", d)
         there = pl.ds(pl.multiple_of(peer * local, 16), local)
-        a = remote(dx_ref.at[there], dx_out.at[d - 1], xs.at[d], xr.at[d], {"seq": peer})
-        b = remote(ctx_ref.at[there], ctx_out.at[:, mine_columns], cs.at[d], cr.at[d], {"seq": peer})
-        seq_copies += [a, b]
+        copy = remote(ctx_ref.at[there], ctx_out.at[:, mine_columns], cs.at[d], cr.at[d], {"seq": peer})
+        seq_copies.append(copy)
     own = pltpu.make_async_copy(
         ctx_ref.at[pl.ds(pl.multiple_of(me * local, 16), local)], ctx_out.at[:, mine_columns], local_sem
     )
@@ -311,7 +363,21 @@
         s1[i] = product(block, lax.rem(i, fsdp_count))
         copy1(i).start()
 
+    def feature_gradient(peer):
+        part = grad_ref[pl.ds(pl.multiple_of(peer * local, 16), local), :]
+        return nt(part, w_ref[...])
+
+    def copy_dx(d):
+        peer = lax.rem(me + d, seq_count)
+        return remote(sdx.at[d - 1], rdx.at[d - 1], xs.at[d], xr.at[d], {"seq": peer})
+
+    def to_seq(i):
+        d = i + 1
+        sdx[i] = feature_gradient(lax.rem(me + d, seq_count)).astype(BF16)
+        copy_dx(d).start()
+
     loop(2 * fsdp_count, to_core)
+    loop(seq_count - 1, to_seq)
 
     def to_x(d):
         own_part = product(far + core, d)
@@ -323,6 +389,7 @@
             copy.start()
 
     loop(fsdp_count, to_x)
+    normed_gradient[...] = feature_gradient(me)
 
     def arrived(d):
         own_part = product(near + core, d)
@@ -352,12 +419,27 @@
     last = []
     for d in range(1, seq_count):
         peer = ring("seq", d)
-        copy = remote(s4.at[peer], out_ref.at[me], s4s.at[d], s4r.at[d], {"seq": peer})
+        copy = remote(s4.at[peer], r4.at[me], s4s.at[d], s4r.at[d], {"seq": peer})
         copy.start()
         last.append(copy)
-    out_ref[me] = s4[me]
+    r4[me] = s4[me]
+
+    def from_seq(i):
+        copy_dx(i + 1).wait_recv()
+        normed_gradient[...] += rdx[i].astype(F32)
+
+    loop(seq_count - 1, from_seq)
+    gradient = normed_gradient[...]
+    standard, inv_std = standardise(frames_ref[...])
+    row_mean = jnp.mean(gradient, axis=1, keepdims=True)
+    projected = jnp.mean(gradient * standard, axis=1, keepdims=True)
+    input_out[...] = inv_std * (gradient - row_mean - standard * projected)
     for copy in last:
         copy.wait()
+    for p in range(seq_count):
+        for kind in range(3):
+            column = (kind * seq_count + p) * gw
+            out_ref[:, column : column + gw] = r4[p, :, kind * gw : (kind + 1) * gw]
     for copy in seq_copies:
         copy.wait()
     own.wait()
@@ -373,12 +455,17 @@
         for copy in copy3(d):
             copy.wait_send()
 
+    def drain_dx(i):
+        copy_dx(i + 1).wait_send()
+
+    loop(seq_count - 1, drain_dx)
     loop(2 * fsdp_count, drain1)
     loop(fsdp_count, drain2)
     loop(fsdp_count - 1, drain3)
 
 
-def reduce(normed_t, grad, dx, ctx, seq_count, fsdp_count, local):
+def reduce(normed_t, grad, w_all, frames, ctx, seq_count, fsdp_count):
+    local = frames.shape[0]
     features, columns = normed_t.shape[0], grad.shape[1]
     gw = columns // 3
     rows = features // (4 * fsdp_count)
@@ -391,12 +478,12 @@
     return pl.pallas_call(
         functools.partial(reduce_kernel, seq_count, fsdp_count),
         out_shape=(
-            jax.ShapeDtypeStruct((seq_count, final, columns), F32),
-            jax.ShapeDtypeStruct((max(seq_count - 1, 1), local, features), BF16),
+            jax.ShapeDtypeStruct((final, seq_count * columns), F32),
+            jax.ShapeDtypeStruct((local, features), F32),
             jax.ShapeDtypeStruct((local, seq_count * gw), BF16),
         ),
-        in_specs=[vmem, vmem, any_spec, any_spec],
-        out_specs=(vmem, any_spec, any_spec),
+        in_specs=[vmem, vmem, vmem, vmem, any_spec],
+        out_specs=(vmem, vmem, any_spec),
         scratch_shapes=[
             pltpu.VMEM((2 * n, rows, columns), F32),
             pltpu.VMEM((2 * n, rows, columns), F32),
@@ -410,6 +497,10 @@
             pltpu.VMEM((n, 1, columns), F32),
             pltpu.VMEM((rows, columns), F32),
             pltpu.VMEM((seq_count, final, columns), F32),
+            pltpu.VMEM((seq_count, final, columns), F32),
+            pltpu.VMEM((seq_count - 1, local, features), BF16),
+            pltpu.VMEM((seq_count - 1, local, features), BF16),
+            pltpu.VMEM((local, features), F32),
             dma,
         ]
         + [dma((2 * n,))] * 2
@@ -419,7 +510,7 @@
             collective_id=1, has_side_effects=True, vmem_limit_bytes=VMEM_BYTES
         ),
         name="reduce_gradients",
-    )(normed_t, grad, dx, ctx)
+    )(normed_t, grad, w_all, frames, ctx)
 
 
 def standardise(rows):
@@ -434,29 +525,13 @@
     upstream = cotangent[0]
     seq_count = lax.axis_size("seq")
     fsdp_count = lax.axis_size("fsdp")
-    me = lax.axis_index("seq")
-    local, features = inputs.shape
     gw = HEADS // seq_count * HD
-    w_mine = lax.dynamic_index_in_dim(
-        projection.reshape(-1, 3, seq_count, gw), me, axis=2, keepdims=False
-    ).reshape(-1, 3 * gw)
-    w_all, x_all, c_all = gather(w_mine, inputs, upstream, seq_count, fsdp_count, gw)
-    normed = standardise(x_all)[0].astype(BF16)
+    normed_mine = standardise(inputs)[0].astype(BF16)
+    w_all, normed, c_all = gather(projection, normed_mine, upstream, seq_count, fsdp_count, gw)
     packed = jnp.dot(normed, w_all, preferred_element_type=F32).astype(BF16)
     ctx, grad = attention(lengths, packed, c_all, gw)
-    partial = nt(grad, w_all)
-    out, dx, context = reduce(
-        normed.T, grad, partial.astype(BF16), ctx, seq_count, fsdp_count, local
-    )
-    normed_gradient = lax.dynamic_slice_in_dim(partial, me * local, local, 0)
-    for d in range(seq_count - 1):
-        normed_gradient = normed_gradient + dx[d].astype(F32)
-    standard, inv_std = standardise(inputs)
-    row_mean = jnp.mean(normed_gradient, axis=1, keepdims=True)
-    projected = jnp.mean(normed_gradient * standard, axis=1, keepdims=True)
-    input_gradient = inv_std * (normed_gradient - row_mean - standard * projected)
-    projection_gradient = (
-        out.reshape(seq_count, -1, 3, gw).transpose(1, 2, 0, 3).reshape(-1, 3 * seq_count * gw)
+    projection_gradient, input_gradient, context = reduce(
+        normed.T, grad, w_all, inputs, ctx, seq_count, fsdp_count
     )
     return (context[None], input_gradient[None], projection_gradient)
 

time: 166 us -> 127 us (0.77)
  Pallas kernels: 136 us -> 107 us
  local copies, waits for them, and re-layouts: 10.4 us -> 6.99 us
  matrix products: 9.54 us -> 6.57 us
  other arithmetic: 6.63 us -> 3.97 us
    pallas_call x1, Pallas kernels: 74.1 us -> 39.2 us  [gather(): pl.pallas_call(functools.partial(gather_kernel, seq_count, fsdp_count), o...]
    dot_general x1 -> x0, matrix products: 5.79 us -> none  [nt(): lax.dot_general(a, b, (((1,), (1,)), ((), ())), preferred_element_type=F32)]
    pallas_call x1, Pallas kernels: 49.6 us -> 54.7 us  [reduce(): pl.pallas_call(functools.partial(reduce_kernel, seq_count, fsdp_count), o...]
    reshape x3 -> x0, local copies, waits for them, and re-layouts: 3.2 us -> none  [the longest x2 1.75 us: body(): out.reshape(seq_count, -1, 3, gw).transpose(1, 2, 0, 3)]
    dot_general x1, matrix products: 3.74 us -> 6.57 us  [body(): packed = jnp.dot(normed, w_all, preferred_element_type=F32).astype(BF16)]
    reduce_sum x1 -> x0, other arithmetic: 2.05 us -> none  [body(): row_mean = jnp.mean(normed_gradient, axis=1, keepdims=True)]
    broadcast_in_dim x1 -> x0, other arithmetic: 1.71 us -> none  [body(): return (context[None], input_gradient[None], projection_gradient)]
    unnamed x14 -> x9, local copies, waits for them, and re-layouts: 4.89 us -> 5.41 us
where the time goes in v2:
time: 127 us; the launch traced here: 126 us
  Pallas kernels  107 us (84%)
  local copies, waits for them, and re-layouts  6.99 us (6%)
  matrix products  6.57 us (5%)
  other arithmetic  3.97 us (3%)
  between operations  1.4 us (1%)
    pallas_call x1, Pallas kernels, reduce(): pl.pallas_call(functools.partial(reduce_kernel, seq_count, fsdp_count), o...  54.7 us
    pallas_call x1, Pallas kernels, gather(): pl.pallas_call(functools.partial(gather_kernel, seq_count, fsdp_count), o...  39.2 us
    pallas_call x1, Pallas kernels, attention(): pl.pallas_call(attention_kernel, grid=(pairs, total // block), out_shape=...  12.7 us
    dot_general x1, matrix products, body(): packed = jnp.dot(normed, w_all, preferred_element_type=F32).astype(BF16)  6.57 us
    unnamed x9, local copies, waits for them, and re-layouts  5.41 us

profile of v2, /device:TPU:0, one launch (start us, length us, event | category | flops | bytes accessed | tf_op | source)
XLA Modules:
  0.0 125.5 jit_solution(13213158651943548099)
XLA Ops:
  0.6 0.0 copy-start
  1.4 1.3 %convert_reduce_fusion = f32[256]{0:T(256)S(1)} fusion(bf16[1,256,1536]{2,1,0:T(8,128)(2,1)} %param.4), kind=kLoop, calls=%fused_computation.2 | loop fusion | flops 786176 | bytes 787456 | tf_op jit(solution)/shard_map/reduce_sum | solution.py:518
  2.7 1.5 %fusion.2 = f32[256]{0:T(256)S(1)} fusion(f32[256]{0:T(256)S(1)} %broadcast_multiply_fusion, bf16[1,256,1536]{2,1,0:T(8,128)(2,1)} %param.4), kind=kLoop, calls=%fused_computation.5 | loop fusion | flops 1572608 | bytes 788480 | tf_op jit(solution)/shard_map/reduce_sum | solution.py:519
  4.2 0.0 copy-done
  4.2 1.2 fusion.3.x_ref
  5.4 39.2 %gather_inputs.1 = (bf16[1536,1536]{1,0:T(8,128)(2,1)}, bf16[512,1536]{1,0:T(8,128)(2,1)}, bf16[512,512]{1,0:T(8,128)(2,1)}) custom-call(bf16[384,3072]{1,0:T(8,128)(2,1)} %w_ref.1, bf16[256,1536]{1,0:T(8,128)(2,1)} %fusion.3.x_ref, bf16[256,1024]{1,0:T(8,128)(2,1)} %bitcast.13), custom_call_target="tpu_custom_call" | custom-call | tf_op jit(solution)/shard_map/gather_inputs/pallas_call | solution.py:172
  44.6 6.6 %convolution_convert_fusion.q_ref.k_ref.v_ref = bf16[512,1536]{1,0:T(8,128)(2,1)} fusion(bf16[512,1536]{1,0:T(8,128)(2,1)} %get-tuple-element.11, bf16[1536,1536]{1,0:T(8,128)(2,1)} %get-tuple-element.12.w_ref), kind=kOutput, calls=%fused_computation | convolution fusion | flops 2416705536 | bytes 7864320 | tf_op jit(solution)/shard_map/dot_general | solution.py:531
  51.1 0.0 copy-start.1
  51.1 12.7 %attention.1 = (bf16[512,512]{1,0:T(8,128)(2,1)}, bf16[512,1536]{1,0:T(8,128)(2,1)}) custom-call(s32[1]{0:T(128)S(6)} %copy.11.len_ref, bf16[512,1536]{1,0:T(8,128)(2,1)} %convolution_convert_fusion.q_ref.k_ref.v_ref, bf16[512,1536]{1,0:T(8,128)(2,1)} %convolution_convert_fusion.q_ref.k_ref.v_ref, ...), custom_call_target="tpu_custom_call" | custom-call | flops 1610612736 | bytes 4194304 | tf_op jit(solution)/shard_map/attention/pallas_call | solution.py:262
  63.8 0.0 copy-done.1
  63.8 1.6 %copy.7 = bf16[512,1536]{0,1:T(8,128)(2,1)} copy(bf16[512,1536]{1,0:T(8,128)(2,1)S(1)} %copy-done.1) | data formatting | bytes 3145728 | tf_op jit(solution)/shard_map/gather_inputs/pallas_call | solution.py:172
  65.4 54.7 %reduce_gradients.1 = (f32[48,3072]{1,0:T(8,128)}, f32[256,1536]{1,0:T(8,128)}, bf16[256,1024]{1,0:T(8,128)(2,1)}) custom-call(bf16[1536,512]{1,0:T(8,128)(2,1)} %bitcast.11, bf16[512,1536]{1,0:T(8,128)(2,1)} %get-tuple-element.14.grad_ref, bf16[1536,1536]{1,0:T(8,128)(2,1)} %get-tuple-element.12.w_ref, bf16[256,1536]{1,0:T(8,128)(2,1)} %bitcast.10, ...), custom_call_target="tpu_custom_call" | custom-call | tf_op jit(solution)/shard_map/reduce_gradients/pallas_call | solution.py:478
  120.1 1.9 %copy.12 = bf16[1,256,1024]{2,1,0:T(8,128)(2,1)} copy(bf16[1,256,1024]{2,1,0:T(8,128)(2,1)} %bitcast.14) | data formatting | bytes 1048576
  122.0 0.0 copy-start.2
  122.0 2.7 %copy.13 = f32[1,256,1536]{2,1,0:T(8,128)} copy(f32[1,256,1536]{2,1,0:T(8,128)} %bitcast.12) | data formatting | bytes 3145728
  124.7 0.0 copy-done.2
  124.7 0.8 copy.14
  (2 shorter events, 0.0 us)
Async XLA Ops:
  0.6 3.6 %copy-start = (bf16[1,256,1536]{2,1,0:T(8,128)(2,1)S(1)}, bf16[1,256,1536]{2,1,0:T(8,128)(2,1)}, u32[]{:S(2)}) copy-start(bf16[1,256,1536]{2,1,0:T(8,128)(2,1)} %param.4) | copy-start | bytes 2359300
  51.1 12.7 %copy-start.1 = (bf16[512,1536]{1,0:T(8,128)(2,1)S(1)}, bf16[512,1536]{1,0:T(8,128)(2,1)}, u32[]{:S(2)}) copy-start(bf16[512,1536]{1,0:T(8,128)(2,1)} %get-tuple-element.11) | copy-start | bytes 4718596
  122.0 2.7 %copy-start.2 = (f32[48,3072]{1,0:T(8,128)S(1)}, f32[48,3072]{1,0:T(8,128)}, u32[]{:S(2)}) copy-start(f32[48,3072]{1,0:T(8,128)} %get-tuple-element.24) | copy-start | bytes 1769476
